TPU v7x, 128 devices: a whole 4x4x4 slice. The times are simulated.
128 devices in a mesh: row: 16 (over z, x_lo, core), col: 8 (over x_hi, y).
Axes of the slice: x: 4 (x_hi: 2, x_lo: 2; x = x_hi * 2 + x_lo), y: 4, z: 4, core: 2. Of those that a mesh axis runs over, the one named last changes fastest.
Arguments:
- tile_values: bfloat16 [32768, 128, 128], P(('row', 'col')), may hold values from -0.09375 to 0.09375
- slot_codes: int32 [32768], P(('row', 'col')), may hold values from -1 to 511, as said below
- right_start: float32 [32768, 256], P(('row', 'col')), may hold values from -6 to 6
- left_start: float32 [32768, 256], P(('row', 'col')), may hold values from -6 to 6
- node_diagonal: float32 [32768], P(('row', 'col')), may hold values from 1 to 3
- row_scale: float32 [32768], P(('row', 'col')), may hold values from 0.2 to 15
Outputs:
- right_block: float32 [32768, 256], P(('row', 'col'))
- left_block: float32 [32768, 256], P(('row', 'col'))
- projections: float32 [2, 256, 256], replicated
Inputs may be any that keep to these rules, and one draw needn't show every extreme that they name: `slot_codes`: slot (s, p, c) carries a tile that device s extracted for owner p; its code is -1 (empty) or a position a 32 + b in p's block grid of 16 x 2 * 16 places. The codes of one owner's live slots over all sources are distinct, so an owner receives at most 128 live tiles, and some owner receives exactly 128. A source fills at most 2 slots for one owner, and some source fills all 2.
All inputs are finite; a program needn't handle non-finite values.
Results may differ from a plain program's by a relative error of at most 0.002.
Values may be sent and summed in bfloat16 or wider, within the bound.
A program may use at most 128 MiB of HBM per device.

v0:
```python
import jax
import jax.numpy as jnp
from jax import lax
from jax.sharding import PartitionSpec as P

ITERS = 2
epsilon = 1e-06


def slot_product(slot_tiles, pick_keys, sum_keys, blocks, key_count, transposed):
    tile_rows = slot_tiles.shape[1]
    port_count = blocks.shape[2]
    slot_total = slot_tiles.shape[0]
    groups = 4
    grouped_tiles = slot_tiles.reshape(groups, slot_total // groups, tile_rows, tile_rows)
    grouped_pick = pick_keys.reshape(groups, slot_total // groups)
    grouped_sum = sum_keys.reshape(groups, slot_total // groups)
    form = "syx,syp->sxp" if transposed else "sxy,syp->sxp"

    def accumulate(summed, group):
        group_tiles, group_pick, group_sum = group
        picked = blocks[group_pick]
        contrib = jnp.einsum(form, group_tiles, picked, preferred_element_type=jnp.float32)
        onehot = (group_sum[:, None] == jnp.arange(key_count)[None, :]).astype(jnp.float32)
        added = jnp.einsum("sn,sxp->nxp", onehot, contrib, precision=lax.Precision.HIGHEST)
        return (summed + added, None)

    start = jnp.zeros((key_count, tile_rows, port_count), jnp.float32)
    summed, _ = lax.scan(accumulate, start, (grouped_tiles, grouped_pick, grouped_sum))
    return summed.reshape(key_count * tile_rows, port_count)


def local(tile_values, slot_codes, right_start, left_start, node_diagonal, row_scale):
    row_size = lax.axis_size("row")
    col_size = lax.axis_size("col")
    owners = row_size * col_size
    tile_rows = tile_values.shape[1]
    port_count = right_start.shape[1]
    order_rows = right_start.shape[0] * owners
    grid_rows = 2 * col_size
    grid_cols = 2 * row_size
    got_tiles, got_codes = (
        lax.all_to_all(tile_values, ("row", "col"), split_axis=0, concat_axis=0, tiled=True),
        lax.all_to_all(slot_codes, ("row", "col"), split_axis=0, concat_axis=0, tiled=True),
    )
    live = got_codes >= 0
    block_row = got_codes // grid_cols
    block_col = got_codes % grid_cols
    row_sum_key = jnp.where(live, block_row, grid_rows)
    col_pick_key = jnp.where(live, block_col, 0)
    row_pick_key = jnp.where(live, block_row, 0)
    col_sum_key = jnp.where(live, block_col, grid_cols)
    scale_col = row_scale[:, None]
    diag_col = node_diagonal[:, None]
    right_vec = right_start
    left_vec = right_start + left_start
    stored = []
    for turn in range(ITERS):
        right_bf = right_vec.astype(jnp.bfloat16)
        scaled_left = scale_col * left_vec
        left_bf = scaled_left.astype(jnp.bfloat16)
        right_cols = lax.all_gather(right_bf, "row", axis=0, tiled=True)
        left_rows = lax.all_gather(left_bf, "col", axis=0, tiled=True)
        right_blocks = right_cols.reshape(grid_cols, tile_rows, port_count)
        right_part = slot_product(
            got_tiles, col_pick_key, row_sum_key, right_blocks, grid_rows, False
        )
        blocks = left_rows.reshape(grid_rows, tile_rows, port_count)
        left_part = slot_product(got_tiles, row_pick_key, col_sum_key, blocks, grid_cols, True)
        right_prod = lax.psum_scatter(right_part, "col", scatter_dimension=0, tiled=True)
        left_prod = lax.psum_scatter(left_part, "row", scatter_dimension=0, tiled=True)
        right_new = scale_col * (right_prod + diag_col * right_vec)
        left_new = left_prod + diag_col * scaled_left
        local_proj = jnp.dot(left_vec.T, right_new, precision=lax.Precision.HIGHEST)
        project = lax.psum(local_proj, ("row", "col")) / order_rows
        right_rest = right_new - jnp.dot(right_vec, project, precision=lax.Precision.HIGHEST)
        left_rest = left_new - jnp.dot(left_vec, project.T, precision=lax.Precision.HIGHEST)
        right_sq, left_sq = lax.psum(
            (jnp.sum(right_rest * right_rest, axis=0), jnp.sum(left_rest * left_rest, axis=0)),
            ("row", "col"),
        )
        right_vec = right_rest / jnp.sqrt(right_sq / order_rows + epsilon)[None, :]
        left_vec = left_rest / jnp.sqrt(left_sq / order_rows + epsilon)[None, :]
        stored.append(project)
    return (right_vec, left_vec, jnp.stack(stored))


def solution(mesh):
    return jax.shard_map(
        local,
        mesh=mesh,
        in_specs=(
            P(("row", "col"), None, None),
            P(("row", "col")),
            P(("row", "col"), None),
            P(("row", "col"), None),
            P(("row", "col")),
            P(("row", "col")),
        ),
        out_specs=(P(("row", "col"), None), P(("row", "col"), None), P()),
        check_vma=False,
    )
```

profile of v0, /device:TPU:1, one launch (start us, length us, event | category | flops | bytes accessed | tf_op | source)
XLA Modules:
  0.0 1186.2 jit_solution(6084935444073180689)
XLA Ops:
  8.0 21.1 %all_to_all.17 = s32[128,2,1]{1,2,0:T(1,128)S(1)} all-to-all(s32[128,2,1]{1,2,0:T(1,128)S(1)} %bitcast.149), channel_id=1, replica_groups=mesh['row'=16,'col'=8] {'row','col'}, dimensions={0} | all-to-all | bytes 2048 | tf_op jit(solution)/shard_map/all_to_all | solution.py:44
  36.8 112.9 %all-gather.5.cloned.1.call-done = bf16[4096,256]{1,0:T(8,128)(2,1)} async-done(((bf16[256,256]{1,0:T(8,128)(2,1)}), bf16[4096,256]{1,0:T(8,128)(2,1)}) %all-gather.5.cloned.1.call-update) | async-done | bytes 2097168 | tf_op jit(solution)/shard_map/all_gather | solution.py:62
  149.7 90.1 %while.44 = (s32[]{:T(128)}, f32[16,128,256]{2,0,1:T(8,128)S(1)}, s32[4,64]{1,0:T(4,128)S(1)}, bf16[4,64,128,128]{3,2,1,0:T(8,128)(2,1)}, s32[4,64]{1,0:T(4,128)...) while((s32[]{:T(128)}, f32[16,128,256]{2,0,1:T(8,128)S(1)}, ...), condition=%wide.region_1.2_spmd.clone, body=%wide.region_0.1_spmd.clone.sunk | while | flops 940574912 | bytes 35658084 | solution.py:29
  255.1 61.6 %reduce-scatter.5.cloned.1.call-done = f32[256,256]{1,0:T(8,128)} async-done(((f32[2048,256]{1,0:T(8,128)}), f32[256,256]{1,0:T(8,128)}) %reduce-scatter.5.cloned.1.call-update) | async-done | bytes 262160 | tf_op jit(solution)/shard_map/reduce_scatter | solution.py:70
  319.7 45.1 %all-gather.9.cloned.1.call-done = bf16[2048,256]{1,0:T(8,128)(2,1)} async-done(((bf16[256,256]{1,0:T(8,128)(2,1)}), bf16[2048,256]{1,0:T(8,128)(2,1)}) %all-gather.9.cloned.1.call-update) | async-done | bytes 1048592 | tf_op jit(solution)/shard_map/all_gather | solution.py:63
  364.8 101.9 %while.46 = (s32[]{:T(128)}, f32[32,128,256]{2,0,1:T(8,128)}, s32[4,64]{1,0:T(4,128)S(1)}, bf16[4,64,128,128]{2,3,1,0:T(8,128)(2,1)}, s32[4,64]{1,0:T(4,128)S(1)...) while((s32[]{:T(128)}, f32[32,128,256]{2,0,1:T(8,128)}, s32[4,64]{1,0:T(4,128)S(1)}, ...), condition=%wide.region_10.11_spmd.clone, body=%wide.region_9.10_spmd.clone.sunk | while | flops 1344277760 | bytes 39852388 | solution.py:29
  376.1 13.3 %select_add_fusion.10 = f32[32,128,256]{2,0,1:T(8,128)} fusion(f32[32,128,256]{2,0,1:T(8,128)} %get-tuple-element.481, f32[64,128,256]{2,1,0:T(8,128)} %fusion.131, pred[]{:T(512)S(6)} %compare.21, s32[64]{0:T(128)S(1)} %fusion.132), kind=kOutput, calls=%fused_computation.40.clone.1 | convolution fusion | flops 807405568 | bytes 16777472 | tf_op jit(solution)/shard_map/while/body/eval_jaxpr/sn,sxp->nxp/dot_general | solution.py:25
  400.7 14.4 %select_add_fusion.10 = f32[32,128,256]{2,0,1:T(8,128)} fusion(f32[32,128,256]{2,0,1:T(8,128)} %get-tuple-element.481, f32[64,128,256]{2,1,0:T(8,128)} %fusion.131, pred[]{:T(512)S(6)} %compare.21, s32[64]{0:T(128)S(1)} %fusion.132), kind=kOutput, calls=%fused_computation.40.clone.1 | convolution fusion | flops 807405568 | bytes 16777472 | tf_op jit(solution)/shard_map/while/body/eval_jaxpr/sn,sxp->nxp/dot_general | solution.py:25
  426.4 14.4 %select_add_fusion.10 = f32[32,128,256]{2,0,1:T(8,128)} fusion(f32[32,128,256]{2,0,1:T(8,128)} %get-tuple-element.481, f32[64,128,256]{2,1,0:T(8,128)} %fusion.131, pred[]{:T(512)S(6)} %compare.21, s32[64]{0:T(128)S(1)} %fusion.132), kind=kOutput, calls=%fused_computation.40.clone.1 | convolution fusion | flops 807405568 | bytes 16777472 | tf_op jit(solution)/shard_map/while/body/eval_jaxpr/sn,sxp->nxp/dot_general | solution.py:25
  452.1 14.4 %select_add_fusion.10 = f32[32,128,256]{2,0,1:T(8,128)} fusion(f32[32,128,256]{2,0,1:T(8,128)} %get-tuple-element.481, f32[64,128,256]{2,1,0:T(8,128)} %fusion.131, pred[]{:T(512)S(6)} %compare.21, s32[64]{0:T(128)S(1)} %fusion.132), kind=kOutput, calls=%fused_computation.40.clone.1 | convolution fusion | flops 807405568 | bytes 16777472 | tf_op jit(solution)/shard_map/while/body/eval_jaxpr/sn,sxp->nxp/dot_general | solution.py:25
  473.4 38.5 %all-reduce.5.cloned.1.call-done = f32[256,256]{1,0:T(8,128)} async-done(((f32[256,256]{1,0:T(8,128)}), f32[256,256]{1,0:T(8,128)}) %all-reduce.5.cloned.1.call-update) | async-done | bytes 262160 | tf_op jit(solution)/shard_map/psum | solution.py:75
  513.2 66.1 %reduce-scatter.9.cloned.1.call-done = f32[256,256]{1,0:T(8,128)} async-done(((f32[4096,256]{1,0:T(8,128)}), f32[256,256]{1,0:T(8,128)}) %reduce-scatter.9.cloned.1.call-update) | async-done | bytes 262160 | tf_op jit(solution)/shard_map/reduce_scatter | solution.py:71
  580.8 67.3 %all-reduce.1 = (f32[256]{0:T(256)S(1)}, f32[256]{0:T(256)S(1)}) all-reduce(f32[256]{0:T(256)S(1)} %get-tuple-element.290, f32[256]{0:T(256)S(1)} %get-tuple-element.292), channel_id=1, replica_groups=mesh['row'=16,'col'=8] {'row','col'}, use_global_device_ids=true, to_apply=%region_5.6 | all-reduce | flops 512 | bytes 4096 | tf_op jit(solution)/shard_map/psum | solution.py:78
  648.8 31.3 %all-gather.7.cloned.1.call-done = bf16[4096,256]{1,0:T(8,128)(2,1)} async-done(((bf16[256,256]{1,0:T(8,128)(2,1)}), bf16[4096,256]{1,0:T(8,128)(2,1)}) %all-gather.7.cloned.1.call-update) | async-done | bytes 2097168 | tf_op jit(solution)/shard_map/all_gather | solution.py:62
  680.1 90.2 %while.45 = (s32[]{:T(128)}, f32[16,128,256]{2,0,1:T(8,128)S(1)}, s32[4,64]{1,0:T(4,128)S(1)}, bf16[4,64,128,128]{3,2,1,0:T(8,128)(2,1)}, s32[4,64]{1,0:T(4,128)...) while((s32[]{:T(128)}, f32[16,128,256]{2,0,1:T(8,128)S(1)}, ...), condition=%wide.region_7.8_spmd.clone, body=%wide.region_6.7_spmd.clone.sunk | while | flops 940574912 | bytes 35658084 | solution.py:29
  773.9 72.2 %reduce-scatter.7.cloned.1.call-done = f32[256,256]{1,0:T(8,128)} async-done(((f32[2048,256]{1,0:T(8,128)}), f32[256,256]{1,0:T(8,128)}) %reduce-scatter.7.cloned.1.call-update) | async-done | bytes 262160 | tf_op jit(solution)/shard_map/reduce_scatter | solution.py:70
  848.5 45.6 %all-gather.11.cloned.1.call-done = bf16[2048,256]{1,0:T(8,128)(2,1)} async-done(((bf16[256,256]{1,0:T(8,128)(2,1)}), bf16[2048,256]{1,0:T(8,128)(2,1)}) %all-gather.11.cloned.1.call-update) | async-done | bytes 1048592 | tf_op jit(solution)/shard_map/all_gather | solution.py:63
  894.1 102.2 %while.47 = (s32[]{:T(128)}, f32[32,128,256]{2,0,1:T(8,128)}, s32[4,64]{1,0:T(4,128)S(1)}, bf16[4,64,128,128]{2,3,1,0:T(8,128)(2,1)}, s32[4,64]{1,0:T(4,128)S(1)...) while((s32[]{:T(128)}, f32[32,128,256]{2,0,1:T(8,128)}, s32[4,64]{1,0:T(4,128)S(1)}, ...), condition=%wide.region_18.19_spmd.clone, body=%wide.region_17.18_spmd.clone.sunk | while | flops 1344277760 | bytes 39852388 | solution.py:29
  930.2 14.4 %select_add_fusion.11 = f32[32,128,256]{2,0,1:T(8,128)} fusion(f32[32,128,256]{2,0,1:T(8,128)} %get-tuple-element.529, f32[64,128,256]{2,1,0:T(8,128)} %fusion.138, pred[]{:T(512)S(6)} %compare.22, s32[64]{0:T(128)S(1)} %fusion.139), kind=kOutput, calls=%fused_computation.57.clone.1 | convolution fusion | flops 807405568 | bytes 16777472 | tf_op jit(solution)/shard_map/while/body/eval_jaxpr/sn,sxp->nxp/dot_general | solution.py:25
  956.0 14.4 %select_add_fusion.11 = f32[32,128,256]{2,0,1:T(8,128)} fusion(f32[32,128,256]{2,0,1:T(8,128)} %get-tuple-element.529, f32[64,128,256]{2,1,0:T(8,128)} %fusion.138, pred[]{:T(512)S(6)} %compare.22, s32[64]{0:T(128)S(1)} %fusion.139), kind=kOutput, calls=%fused_computation.57.clone.1 | convolution fusion | flops 807405568 | bytes 16777472 | tf_op jit(solution)/shard_map/while/body/eval_jaxpr/sn,sxp->nxp/dot_general | solution.py:25
  981.7 14.4 %select_add_fusion.11 = f32[32,128,256]{2,0,1:T(8,128)} fusion(f32[32,128,256]{2,0,1:T(8,128)} %get-tuple-element.529, f32[64,128,256]{2,1,0:T(8,128)} %fusion.138, pred[]{:T(512)S(6)} %compare.22, s32[64]{0:T(128)S(1)} %fusion.139), kind=kOutput, calls=%fused_computation.57.clone.1 | convolution fusion | flops 807405568 | bytes 16777472 | tf_op jit(solution)/shard_map/while/body/eval_jaxpr/sn,sxp->nxp/dot_general | solution.py:25
  1003.9 37.4 %all-reduce.7.cloned.1.call-done = f32[256,256]{1,0:T(8,128)} async-done(((f32[256,256]{1,0:T(8,128)}), f32[256,256]{1,0:T(8,128)}) %all-reduce.7.cloned.1.call-update) | async-done | bytes 262160 | tf_op jit(solution)/shard_map/psum | solution.py:75
  1044.5 64.3 %reduce-scatter.11.cloned.1.call-done = f32[256,256]{1,0:T(8,128)} async-done(((f32[4096,256]{1,0:T(8,128)}), f32[256,256]{1,0:T(8,128)}) %reduce-scatter.11.cloned.1.call-update) | async-done | bytes 262160 | tf_op jit(solution)/shard_map/reduce_scatter | solution.py:71
  1110.2 67.3 %all-reduce = (f32[256]{0:T(256)S(1)}, f32[256]{0:T(256)S(1)}) all-reduce(f32[256]{0:T(256)S(1)} %get-tuple-element.294, f32[256]{0:T(256)S(1)} %get-tuple-element.296), channel_id=1, replica_groups=mesh['row'=16,'col'=8] {'row','col'}, use_global_device_ids=true, to_apply=%region_16.17 | all-reduce | flops 512 | bytes 4096 | tf_op jit(solution)/shard_map/psum | solution.py:78
  (156 shorter events, 340.1 us)
Async XLA Ops:
  29.1 5.4 copy-start.1
  29.1 5.4 copy-start.3
  29.1 5.4 copy-start.4
  29.1 120.6 %all-to-all-start.1 = ((bf16[256,128,128]{2,1,0:T(8,128)(2,1)}), bf16[256,128,128]{2,1,0:T(8,128)(2,1)}, u32[]{:S(2)}, u32[]{:S(2)}) async-start(bf16[256,128,128]{2,1,0:T(8,128)(2,1)} %param.14), calls=%async_computation.1 | async-start | bytes 16777216 | tf_op jit(solution)/shard_map/all_to_all | solution.py:43
  34.4 115.3 %all-gather.5.cloned.1.call-start = ((), (), s32[]{:S(2)}) async-start(), calls=%async_computation.6 | async-start | bytes 2228224 | tf_op jit(solution)/shard_map/all_gather | solution.py:62
  35.3 281.5 %reduce-scatter.5.cloned.1.call-start = ((), (), s32[]{:S(2)}) async-start(), calls=%async_computation.7 | async-start | bytes 2359296 | tf_op jit(solution)/shard_map/reduce_scatter | solution.py:70
  242.3 122.5 %all-gather.9.cloned.1.call-start = ((), (), s32[]{:S(2)}) async-start(), calls=%async_computation.11 | async-start | bytes 1179648 | tf_op jit(solution)/shard_map/all_gather | solution.py:63
  243.1 268.8 %all-reduce.5.cloned.1.call-start = ((), (), s32[]{:S(2)}) async-start(), calls=%async_computation.8 | async-start | bytes 524288 | tf_op jit(solution)/shard_map/psum | solution.py:75
  243.1 73.6 %copy-start.5 = (f32[256]{0:T(256)S(1)}, f32[256]{0:T(256)}, u32[]{:S(2)}) copy-start(f32[256]{0:T(256)} %param.18) | copy-start | bytes 3076
  319.1 260.2 %reduce-scatter.9.cloned.1.call-start = ((), (), s32[]{:S(2)}) async-start(), calls=%async_computation.12 | async-start | bytes 4456448 | tf_op jit(solution)/shard_map/reduce_scatter | solution.py:71
  473.3 38.6 %copy-start.2 = (f32[256,256]{1,0:T(8,128)S(1)}, f32[256,256]{1,0:T(8,128)}, u32[]{:S(2)}) copy-start(f32[256,256]{1,0:T(8,128)} %reduce-scatter.5.cloned.1.call-done) | copy-start | bytes 786436
  473.3 206.8 %all-gather.7.cloned.1.call-start = ((), (), s32[]{:S(2)}) async-start(), calls=%async_computation.9 | async-start | bytes 2228224 | tf_op jit(solution)/shard_map/all_gather | solution.py:62
  648.8 197.3 %reduce-scatter.7.cloned.1.call-start = ((), (), s32[]{:S(2)}) async-start(), calls=%async_computation.10 | async-start | bytes 2359296 | tf_op jit(solution)/shard_map/reduce_scatter | solution.py:70
  773.0 121.1 %all-gather.11.cloned.1.call-start = ((), (), s32[]{:S(2)}) async-start(), calls=%async_computation.14 | async-start | bytes 1179648 | tf_op jit(solution)/shard_map/all_gather | solution.py:63
  773.8 267.5 %all-reduce.7.cloned.1.call-start = ((), (), s32[]{:S(2)}) async-start(), calls=%async_computation.13 | async-start | bytes 524288 | tf_op jit(solution)/shard_map/psum | solution.py:75
  848.4 260.3 %reduce-scatter.11.cloned.1.call-start = ((), (), s32[]{:S(2)}) async-start(), calls=%async_computation.15 | async-start | bytes 4456448 | tf_op jit(solution)/shard_map/reduce_scatter | solution.py:71
  1002.9 0.9 copy-start
  1002.9 40.2 %copy-start.6 = (f32[256,256]{1,0:T(8,128)S(1)}, f32[256,256]{1,0:T(8,128)}, u32[]{:S(2)}) copy-start(f32[256,256]{1,0:T(8,128)} %reduce-scatter.7.cloned.1.call-done) | copy-start | bytes 786436
Sparse Core Ops, SparseCore 0:
  37.5 112.1 all-gather.4
  242.5 74.2 reduce-scatter.4
  319.7 45.0 all-gather.8
  370.0 141.8 all-reduce.4
  514.1 65.1 reduce-scatter.8
  648.9 31.1 all-gather.6
  773.1 72.9 reduce-scatter.6
  849.0 45.0 all-gather.10
  899.4 141.8 all-reduce.6
  1043.5 65.1 reduce-scatter.10
where the time goes:
time: 1200 us; the launch traced here: 1190 us
  waiting for transfers between devices  576 us (48%)
  matrix products  327 us (27%)
  blocking collectives  156 us (13%)
  local copies, waits for them, and re-layouts  99.6 us (8%)
  between operations  14.8 us (1%)
    dot_general x16, matrix products, accumulate(): jnp.einsum('sn,sxp->nxp', onehot, contrib, precision=lax.Precision.HIGHEST)  200 us
    all_gather x2, waiting for transfers between devices, local(): right_cols = lax.all_gather(right_bf, 'row', axis=0, tiled=True)  144 us
    psum x2, blocking collectives, local(): lax.psum((jnp.sum(right_rest * right_rest, axis=0), jnp.sum(left_rest * l...  135 us
    reduce_scatter x2, waiting for transfers between devices, local(): lax.psum_scatter(right_part, 'col', scatter_dimension=0, tiled=True)  134 us
    reduce_scatter x2, waiting for transfers between devices, local(): lax.psum_scatter(left_part, 'row', scatter_dimension=0, tiled=True)  130 us
    dot_general x16, matrix products, accumulate(): jnp.einsum(form, group_tiles, picked, preferred_element_type=jnp.float32)  117 us
    all_gather x2, waiting for transfers between devices, local(): left_rows = lax.all_gather(left_bf, 'col', axis=0, tiled=True)  90.7 us
    psum x2, waiting for transfers between devices, local(): project = lax.psum(local_proj, ('row', 'col')) / order_rows  75.9 us
  transfers between devices with their start and end apart: 11, of which 10 were waited for; matrix products, arithmetic and copies ran while one was open for 20% of the time, Pallas kernels for 0%

commit v1 on v0

--- a/solution.py
+++ b/solution.py
@@ -72,7 +72,7 @@
         right_new = scale_col * (right_prod + diag_col * right_vec)
         left_new = left_prod + diag_col * scaled_left
         local_proj = jnp.dot(left_vec.T, right_new, precision=lax.Precision.HIGHEST)
-        project = lax.psum(local_proj, ("row", "col")) / order_rows
+        project = jnp.sum(lax.all_gather(local_proj, ("row", "col")), axis=0) / order_rows
         right_rest = right_new - jnp.dot(right_vec, project, precision=lax.Precision.HIGHEST)
         left_rest = left_new - jnp.dot(left_vec, project.T, precision=lax.Precision.HIGHEST)
         right_sq, left_sq = lax.psum(

time: 1200 us -> 1610 us (1.34)
  waiting for transfers between devices: 576 us -> 968 us
  other arithmetic: 6.54 us -> 29.6 us
    all_gather x0 -> x2, waiting for transfers between devices: none -> 484 us  [local(): lax.all_gather(local_proj, ('row', 'col'))]
    psum x2 -> x0, waiting for transfers between devices: 75.9 us -> none  [local(): project = lax.psum(local_proj, ('row', 'col')) / order_rows]
    reduce_sum x0 -> x2, other arithmetic: none -> 24 us  [local(): jnp.sum(lax.all_gather(local_proj, ('row', 'col')), axis=0) / order_rows]
  transfers between devices with their start and end apart: 11 -> 11, of which waited for: 10 -> 10; matrix products, arithmetic and copies ran while one was open for 20% -> 16% of each run, Pallas kernels for 0% -> 0%
where the time goes in v1:
time: 1610 us; the launch traced here: 1600 us
  waiting for transfers between devices  968 us (60%)
  matrix products  325 us (20%)
  blocking collectives  157 us (10%)
  local copies, waits for them, and re-layouts  99.4 us (6%)
  other arithmetic  29.6 us (2%)
    all_gather x2, waiting for transfers between devices, local(): lax.all_gather(local_proj, ('row', 'col'))  484 us
    dot_general x16, matrix products, accumulate(): jnp.einsum('sn,sxp->nxp', onehot, contrib, precision=lax.Precision.HIGHEST)  200 us
    reduce_scatter x2, waiting for transfers between devices, local(): lax.psum_scatter(right_part, 'col', scatter_dimension=0, tiled=True)  146 us
    all_gather x2, waiting for transfers between devices, local(): right_cols = lax.all_gather(right_bf, 'row', axis=0, tiled=True)  144 us
    psum x2, blocking collectives, local(): lax.psum((jnp.sum(right_rest * right_rest, axis=0), jnp.sum(left_rest * l...  136 us
    dot_general x16, matrix products, accumulate(): jnp.einsum(form, group_tiles, picked, preferred_element_type=jnp.float32)  117 us
    reduce_scatter x2, waiting for transfers between devices, local(): lax.psum_scatter(left_part, 'row', scatter_dimension=0, tiled=True)  115 us
    all_gather x2, waiting for transfers between devices, local(): left_rows = lax.all_gather(left_bf, 'col', axis=0, tiled=True)  78.7 us
  transfers between devices with their start and end apart: 11, of which 10 were waited for; matrix products, arithmetic and copies ran while one was open for 16% of the time, Pallas kernels for 0%

profile of v1, /device:TPU:1, one launch (start us, length us, event | category | flops | bytes accessed | tf_op | source)
XLA Modules:
  0.0 1601.0 jit_solution(3141025292740353899)
XLA Ops:
  8.0 21.1 %all_to_all.17 = s32[128,2,1]{1,2,0:T(1,128)S(1)} all-to-all(s32[128,2,1]{1,2,0:T(1,128)S(1)} %bitcast.153), channel_id=1, replica_groups=mesh['row'=16,'col'=8] {'row','col'}, dimensions={0} | all-to-all | bytes 2048 | tf_op jit(solution)/shard_map/all_to_all | solution.py:44
  36.8 112.9 %all-gather.9.cloned.1.call-done = bf16[4096,256]{1,0:T(8,128)(2,1)} async-done(((bf16[256,256]{1,0:T(8,128)(2,1)}), bf16[4096,256]{1,0:T(8,128)(2,1)}) %all-gather.9.cloned.1.call-update) | async-done | bytes 2097168 | tf_op jit(solution)/shard_map/all_gather | solution.py:62
  149.7 90.1 %while.44 = (s32[]{:T(128)}, f32[16,128,256]{2,0,1:T(8,128)S(1)}, s32[4,64]{1,0:T(4,128)S(1)}, bf16[4,64,128,128]{3,2,1,0:T(8,128)(2,1)}, s32[4,64]{1,0:T(4,128)...) while((s32[]{:T(128)}, f32[16,128,256]{2,0,1:T(8,128)S(1)}, ...), condition=%wide.region_1.2_spmd.clone, body=%wide.region_0.1_spmd.clone.sunk | while | flops 940574912 | bytes 35658084 | solution.py:29
  243.2 73.6 %reduce-scatter.5.cloned.1.call-done = f32[256,256]{1,0:T(8,128)} async-done(((f32[2048,256]{1,0:T(8,128)}), f32[256,256]{1,0:T(8,128)}) %reduce-scatter.5.cloned.1.call-update) | async-done | bytes 262160 | tf_op jit(solution)/shard_map/reduce_scatter | solution.py:70
  331.7 33.1 %all-gather.13.cloned.1.call-done = bf16[2048,256]{1,0:T(8,128)(2,1)} async-done(((bf16[256,256]{1,0:T(8,128)(2,1)}), bf16[2048,256]{1,0:T(8,128)(2,1)}) %all-gather.13.cloned.1.call-update) | async-done | bytes 1048592 | tf_op jit(solution)/shard_map/all_gather | solution.py:63
  364.8 102.3 %while.46 = (s32[]{:T(128)}, f32[32,128,256]{2,0,1:T(8,128)}, s32[4,64]{1,0:T(4,128)S(1)}, bf16[4,64,128,128]{2,3,1,0:T(8,128)(2,1)}, s32[4,64]{1,0:T(4,128)S(1)...) while((s32[]{:T(128)}, f32[32,128,256]{2,0,1:T(8,128)}, s32[4,64]{1,0:T(4,128)S(1)}, ...), condition=%wide.region_10.11_spmd.clone, body=%wide.region_9.10_spmd.clone.sunk | while | flops 1344277760 | bytes 39852388 | solution.py:29
  376.1 13.3 select_add_fusion.10
  400.7 14.5 select_add_fusion.10
  426.6 14.6 select_add_fusion.10
  452.5 14.5 select_add_fusion.10
  473.9 242.2 %all-gather.17.cloned.1.call-done = f32[32768,256]{1,0:T(8,128)} async-done(((f32[256,256]{1,0:T(8,128)}), f32[32768,256]{1,0:T(8,128)}) %all-gather.17.cloned.1.call-update) | async-done | bytes 33554448 | tf_op jit(solution)/shard_map/all_gather | solution.py:75
  728.6 57.3 %reduce-scatter.9.cloned.1.call-done = f32[256,256]{1,0:T(8,128)} async-done(((f32[4096,256]{1,0:T(8,128)}), f32[256,256]{1,0:T(8,128)}) %reduce-scatter.9.cloned.1.call-update) | async-done | bytes 262160 | tf_op jit(solution)/shard_map/reduce_scatter | solution.py:71
  787.3 67.8 %all-reduce.1 = (f32[256]{0:T(256)S(1)}, f32[256]{0:T(256)S(1)}) all-reduce(f32[256]{0:T(256)S(1)} %get-tuple-element.290, f32[256]{0:T(256)S(1)} %get-tuple-element.292), channel_id=1, replica_groups=mesh['row'=16,'col'=8] {'row','col'}, use_global_device_ids=true, to_apply=%region_5.6 | all-reduce | flops 512 | bytes 4096 | tf_op jit(solution)/shard_map/psum | solution.py:78
  855.9 31.4 %all-gather.11.cloned.1.call-done = bf16[4096,256]{1,0:T(8,128)(2,1)} async-done(((bf16[256,256]{1,0:T(8,128)(2,1)}), bf16[4096,256]{1,0:T(8,128)(2,1)}) %all-gather.11.cloned.1.call-update) | async-done | bytes 2097168 | tf_op jit(solution)/shard_map/all_gather | solution.py:62
  887.3 90.1 %while.45 = (s32[]{:T(128)}, f32[16,128,256]{2,0,1:T(8,128)S(1)}, s32[4,64]{1,0:T(4,128)S(1)}, bf16[4,64,128,128]{3,2,1,0:T(8,128)(2,1)}, s32[4,64]{1,0:T(4,128)...) while((s32[]{:T(128)}, f32[16,128,256]{2,0,1:T(8,128)S(1)}, ...), condition=%wide.region_7.8_spmd.clone, body=%wide.region_6.7_spmd.clone.sunk | while | flops 940574912 | bytes 35658084 | solution.py:29
  980.9 72.2 %reduce-scatter.7.cloned.1.call-done = f32[256,256]{1,0:T(8,128)} async-done(((f32[2048,256]{1,0:T(8,128)}), f32[256,256]{1,0:T(8,128)}) %reduce-scatter.7.cloned.1.call-update) | async-done | bytes 262160 | tf_op jit(solution)/shard_map/reduce_scatter | solution.py:70
  1055.5 45.6 %all-gather.15.cloned.1.call-done = bf16[2048,256]{1,0:T(8,128)(2,1)} async-done(((bf16[256,256]{1,0:T(8,128)(2,1)}), bf16[2048,256]{1,0:T(8,128)(2,1)}) %all-gather.15.cloned.1.call-update) | async-done | bytes 1048592 | tf_op jit(solution)/shard_map/all_gather | solution.py:63
  1101.1 103.2 %while.47 = (s32[]{:T(128)}, f32[32,128,256]{2,0,1:T(8,128)}, s32[4,64]{1,0:T(4,128)S(1)}, bf16[4,64,128,128]{2,3,1,0:T(8,128)(2,1)}, s32[4,64]{1,0:T(4,128)S(1)...) while((s32[]{:T(128)}, f32[32,128,256]{2,0,1:T(8,128)}, s32[4,64]{1,0:T(4,128)S(1)}, ...), condition=%wide.region_18.19_spmd.clone, body=%wide.region_17.18_spmd.clone.sunk | while | flops 1344277760 | bytes 39852388 | solution.py:29
  1137.4 14.5 select_add_fusion.11
  1163.4 14.6 select_add_fusion.11
  1189.5 14.5 select_add_fusion.11
  1211.1 241.5 %all-gather.19.cloned.1.call-done = f32[32768,256]{1,0:T(8,128)} async-done(((f32[256,256]{1,0:T(8,128)}), f32[32768,256]{1,0:T(8,128)}) %all-gather.19.cloned.1.call-update) | async-done | bytes 33554448 | tf_op jit(solution)/shard_map/all_gather | solution.py:75
  1465.0 57.3 %reduce-scatter.11.cloned.1.call-done = f32[256,256]{1,0:T(8,128)} async-done(((f32[4096,256]{1,0:T(8,128)}), f32[256,256]{1,0:T(8,128)}) %reduce-scatter.11.cloned.1.call-update) | async-done | bytes 262160 | tf_op jit(solution)/shard_map/reduce_scatter | solution.py:71
  1523.7 67.7 %all-reduce = (f32[256]{0:T(256)S(1)}, f32[256]{0:T(256)S(1)}) all-reduce(f32[256]{0:T(256)S(1)} %get-tuple-element.294, f32[256]{0:T(256)S(1)} %get-tuple-element.296), channel_id=1, replica_groups=mesh['row'=16,'col'=8] {'row','col'}, use_global_device_ids=true, to_apply=%region_16.17 | all-reduce | flops 512 | bytes 4096 | tf_op jit(solution)/shard_map/psum | solution.py:78
  (156 shorter events, 361.1 us)
Async XLA Ops:
  29.1 5.4 copy-start
  29.1 5.4 copy-start.2
  29.1 5.4 copy-start.3
  29.1 120.6 %all-to-all-start.1 = ((bf16[256,128,128]{2,1,0:T(8,128)(2,1)}), bf16[256,128,128]{2,1,0:T(8,128)(2,1)}, u32[]{:S(2)}, u32[]{:S(2)}) async-start(bf16[256,128,128]{2,1,0:T(8,128)(2,1)} %param.14), calls=%async_computation.1 | async-start | bytes 16777216 | tf_op jit(solution)/shard_map/all_to_all | solution.py:43
  34.4 115.3 %all-gather.9.cloned.1.call-start = ((), (), s32[]{:S(2)}) async-start(), calls=%async_computation.6 | async-start | bytes 2228224 | tf_op jit(solution)/shard_map/all_gather | solution.py:62
  35.3 281.5 %reduce-scatter.5.cloned.1.call-start = ((), (), s32[]{:S(2)}) async-start(), calls=%async_computation.7 | async-start | bytes 2359296 | tf_op jit(solution)/shard_map/reduce_scatter | solution.py:70
  239.8 77.0 %copy-start.4 = (f32[256]{0:T(256)S(1)}, f32[256]{0:T(256)}, u32[]{:S(2)}) copy-start(f32[256]{0:T(256)} %param.18) | copy-start | bytes 3076
  242.4 122.5 %all-gather.13.cloned.1.call-start = ((), (), s32[]{:S(2)}) async-start(), calls=%async_computation.10 | async-start | bytes 1179648 | tf_op jit(solution)/shard_map/all_gather | solution.py:63
  243.1 473.0 %all-gather.17.cloned.1.call-start = ((), (), s32[]{:S(2)}) async-start(), calls=%async_computation.14 | async-start | bytes 33816576 | tf_op jit(solution)/shard_map/all_gather | solution.py:75
  319.2 466.8 %reduce-scatter.9.cloned.1.call-start = ((), (), s32[]{:S(2)}) async-start(), calls=%async_computation.11 | async-start | bytes 4456448 | tf_op jit(solution)/shard_map/reduce_scatter | solution.py:71
  473.9 413.4 %all-gather.11.cloned.1.call-start = ((), (), s32[]{:S(2)}) async-start(), calls=%async_computation.8 | async-start | bytes 2228224 | tf_op jit(solution)/shard_map/all_gather | solution.py:62
  716.2 12.0 copy-start.1
  855.9 197.2 %reduce-scatter.7.cloned.1.call-start = ((), (), s32[]{:S(2)}) async-start(), calls=%async_computation.9 | async-start | bytes 2359296 | tf_op jit(solution)/shard_map/reduce_scatter | solution.py:70
  980.0 121.1 %all-gather.15.cloned.1.call-start = ((), (), s32[]{:S(2)}) async-start(), calls=%async_computation.12 | async-start | bytes 1179648 | tf_op jit(solution)/shard_map/all_gather | solution.py:63
  980.8 471.7 %all-gather.19.cloned.1.call-start = ((), (), s32[]{:S(2)}) async-start(), calls=%async_computation.15 | async-start | bytes 33816576 | tf_op jit(solution)/shard_map/all_gather | solution.py:75
  1055.4 466.9 %reduce-scatter.11.cloned.1.call-start = ((), (), s32[]{:S(2)}) async-start(), calls=%async_computation.13 | async-start | bytes 4456448 | tf_op jit(solution)/shard_map/reduce_scatter | solution.py:71
  1452.6 12.0 copy-start.5
Sparse Core Ops, SparseCore 0:
  37.5 112.1 all-gather.8
  242.5 74.2 reduce-scatter.4
  319.7 45.0 all-gather.12
  367.0 349.1 all-gather.16
  718.4 67.4 reduce-scatter.8
  856.0 31.2 all-gather.10
  980.1 72.9 reduce-scatter.6
  1056.0 45.0 all-gather.14
  1103.4 349.1 all-gather.18
  1454.8 67.4 reduce-scatter.10
